TPU v7x, 32 devices: a whole 2x2x4 slice. The times are simulated.
32 devices in a mesh: groups: 2 (over y), seq: 4 (over x, core), mp: 4 (over z).
Axes of the slice: x: 2, y: 2, z: 4, core: 2. Of those that a mesh axis runs over, the one named last changes fastest.
Arguments:
- queries: bfloat16 [512, 3584], P(('groups', 'seq')), parts along dimension 0, may hold values from -5 to 5
- keys: bfloat16 [512, 512], P(('groups', 'seq')), parts along dimension 0, may hold values from -5 to 5
- values: bfloat16 [512, 512], P(('groups', 'seq')), parts along dimension 0, may hold values from -6 to 6
- hidden_in: bfloat16 [512, 3584], P(('groups', 'seq')), parts along dimension 0, may hold values from -6 to 6
- doc_ids: int32 [512], P(('groups', 'seq')), parts along dimension 0, may hold values from 0 to 7, never falling along the last dimension, each value on 1 to 128 neighbouring positions
- modality: int32 [512], P(('groups', 'seq')), parts along dimension 0, may hold values from 0 to 1, as said below
- input_weights: bfloat16 [3584, 2, 37888], P(None, None, ('seq', 'mp')), may hold values from -0.09375 to 0.09375
- output_weights: bfloat16 [37888, 3584], P(('seq', 'mp')), may hold values from -0.046875 to 0.046875
- norm_gains: float32 [2, 3584], replicated, may hold values from 0.5 to 1.5
Outputs:
- layer_out: bfloat16 [512, 3584], P(('groups', 'seq')), parts along dimension 0
There are 2 independent parts, one for each index of `groups`. A program takes and returns all parts, laid end to end along the dimension named above; an argument that names none is the same for every part. Nothing has to cross between parts.
Inputs may be any that keep to these rules, and one draw needn't show every extreme that they name: Exactly 224 tokens have modality 1; the modality is constant on each aligned block of 16 tokens. `doc_ids`: never falls along the batch; every document has 1 to 128 tokens.
All inputs are finite; a program needn't handle non-finite values.
Results may differ from a plain program's by a relative error of at most 0.0059.
Values may be sent and summed in bfloat16 or wider, within the bound.
A program may use at most 256 MiB of HBM per device.

v0:
```python
import math

import jax
import jax.numpy as jnp
from jax import lax
from jax.sharding import PartitionSpec as P

D = 3584
HEAD_SIZE = 128
FF = 18944


neg_large = -1e30


def swiglu_block(row_block, in_block, out_block):
    unit_count = in_block.shape[2]
    flat_in = in_block.reshape(in_block.shape[0], 2 * unit_count)
    gate_up = jnp.dot(row_block, flat_in, preferred_element_type=jnp.float32)
    activated = (jax.nn.silu(gate_up[:, :unit_count]) * gate_up[:, unit_count:]).astype(
        jnp.bfloat16
    )
    return jnp.dot(activated, out_block, preferred_element_type=jnp.float32)


def body(
    queries, keys, values, hidden_in, doc_ids, modality, input_weights, output_weights, norm_gains
):
    row_count = queries.shape[0]
    group_count = keys.shape[1] // HEAD_SIZE
    head_count = queries.shape[1] // HEAD_SIZE
    heads_per_group = head_count // group_count
    shard_index = lax.axis_index("seq")
    device_index = lax.axis_index(("seq", "mp"))
    query_position = shard_index * row_count + jnp.arange(row_count, dtype=jnp.int32)
    query_by_group = queries.reshape(row_count, group_count, heads_per_group, HEAD_SIZE)
    score_scale = 1.0 / math.sqrt(HEAD_SIZE)
    running_max = jnp.full((row_count, group_count, heads_per_group), neg_large, jnp.float32)
    key_piece = lax.all_gather(keys, "seq", axis=0, tiled=True)
    value_piece = lax.all_gather(values, "seq", axis=0, tiled=True)
    doc_piece = lax.all_gather(doc_ids, "seq", axis=0, tiled=True)
    piece_rows = key_piece.shape[0]
    key_position = jnp.arange(piece_rows, dtype=jnp.int32)
    key_by_group = key_piece.reshape(piece_rows, group_count, HEAD_SIZE)
    value_by_group = value_piece.reshape(piece_rows, group_count, HEAD_SIZE)
    scores = (
        jnp.einsum(
            "rgqd,ngd->rgqn", query_by_group, key_by_group, preferred_element_type=jnp.float32
        )
        * score_scale
    )
    visible = (doc_ids[:, None] == doc_piece[None, :]) & (
        key_position[None, :] <= query_position[:, None]
    )
    visible = visible[:, None, None, :]
    masked = jnp.where(visible, scores, neg_large)
    new_max = jnp.maximum(running_max, jnp.max(masked, axis=-1))
    weights = jnp.where(visible, jnp.exp(masked - new_max[..., None]), 0.0)
    running_sum = jnp.sum(weights, axis=-1)
    low_weights = weights.astype(jnp.bfloat16)
    weighted = jnp.einsum(
        "rgqn,ngd->rgqd", low_weights, value_by_group, preferred_element_type=jnp.float32
    )
    running_max, running_sum, weighted = (new_max, running_sum, weighted)
    attended_output = (weighted / running_sum[..., None]).reshape(row_count, head_count * HEAD_SIZE)
    residual = (hidden_in.astype(jnp.float32) + attended_output).astype(jnp.bfloat16)
    residual_wide = residual.astype(jnp.float32)
    mean_square = jnp.mean(residual_wide * residual_wide, axis=-1, keepdims=True)
    row_gain = jnp.where(modality[:, None] == 1, norm_gains[1][None, :], norm_gains[0][None, :])
    normed = (residual_wide * lax.rsqrt(mean_square + 1e-06) * row_gain).astype(jnp.bfloat16)
    all_rows, all_mods = (
        lax.all_gather(normed, "seq", axis=0, tiled=True),
        lax.all_gather(modality, "seq", axis=0, tiled=True),
    )
    total_rows = all_rows.shape[0]
    image_count = 7 * total_rows // 8
    text_count = total_rows - image_count
    by_modality = jnp.argsort(all_mods, stable=True)
    sorted_rows = all_rows[by_modality]
    unit_count = output_weights.shape[0]
    is_image = device_index >= FF // unit_count

    def text_branch():
        text_out = swiglu_block(sorted_rows[:text_count], input_weights, output_weights)
        return jnp.concatenate([text_out, jnp.zeros((image_count, D), jnp.float32)], axis=0)

    def image_branch():
        image_out = swiglu_block(sorted_rows[text_count:], input_weights, output_weights)
        return jnp.concatenate([jnp.zeros((text_count, D), jnp.float32), image_out], axis=0)

    sorted_out = lax.cond(is_image, image_branch, text_branch)
    partial_value = jnp.zeros((total_rows, D), jnp.float32).at[by_modality].set(sorted_out)
    share = lax.psum_scatter(partial_value, ("seq", "mp"), scatter_dimension=0, tiled=True)
    ffn_sums = lax.all_gather(share, "mp", axis=0, tiled=True)
    return (residual_wide + ffn_sums).astype(jnp.bfloat16)


def solution(mesh):
    in_specs = (
        P(("groups", "seq"), None),
        P(("groups", "seq"), None),
        P(("groups", "seq"), None),
        P(("groups", "seq"), None),
        P(("groups", "seq")),
        P(("groups", "seq")),
        P(None, None, ("seq", "mp")),
        P(("seq", "mp"), None),
        P(),
    )
    out_specs = P(("groups", "seq"), None)
    return jax.shard_map(body, mesh=mesh, in_specs=in_specs, out_specs=out_specs, check_vma=False)
```

profile of v0, /device:TPU:0, one launch (start us, length us, event | category | flops | bytes accessed | tf_op | source)
XLA Modules:
  0.0 194.2 jit_solution(5043303240199700661)
XLA Ops:
  6.5 0.7 broadcast_compare_fusion
  7.3 0.9 slice_reduce_fusion.1
  8.2 7.4 %all_gather.19 = bf16[256,512]{1,0:T(8,128)(2,1)S(1)} all-gather(bf16[64,512]{1,0:T(8,128)(2,1)} %param.12), channel_id=1, replica_groups=mesh['groups'=2,'seq'=4,'mp'=4] {'seq'}, dimensions={0}, use_global_device_ids=true | all-gather | bytes 327680 | tf_op jit(solution)/shard_map/all_gather | solution.py:39
  15.6 0.1 copy.19
  15.7 6.1 %all_gather.20 = bf16[256,512]{1,0:T(8,128)(2,1)S(1)} all-gather(bf16[64,512]{1,0:T(8,128)(2,1)} %param.13), channel_id=1, replica_groups=mesh['groups'=2,'seq'=4,'mp'=4] {'seq'}, dimensions={0}, use_global_device_ids=true | all-gather | bytes 327680 | tf_op jit(solution)/shard_map/all_gather | solution.py:40
  21.8 0.1 copy.22
  21.9 1.6 reshape.78
  23.5 0.6 dynamic-slice
  24.8 0.2 dynamic-update-slice.1
  25.0 0.2 dynamic-update-slice
  25.3 4.9 %all-reduce.4 = (s32[256]{0:T(256)S(1)}, s32[256]{0:T(256)S(1)}) all-reduce(s32[256]{0:T(256)S(1)} %dynamic-update-slice.1, s32[256]{0:T(256)S(1)} %dynamic-update-slice), channel_id=1, replica_groups=mesh['groups'=2,'seq'=4,'mp'=4] {'seq'}, use_global_device_ids=true, to_apply=%add.3 | all-reduce | flops 512 | bytes 4096
  30.2 0.1 fusion.32
  30.3 0.5 fusion.16
  30.9 0.8 fusion.18
  31.7 1.2 fusion.17
  32.9 0.5 copy.24
  33.4 0.2 reshape.80
  33.6 0.3 copy-done
  33.9 0.2 fusion.21
  34.1 1.0 fusion.23
  35.1 0.0 reduce-scatter.2.cloned.1.call-start
  35.2 3.2 %sort.17 = (s32[256]{0:T(256)}, s32[256]{0:T(256)S(1)}) sort(s32[256]{0:T(256)S(1)} %get-tuple-element.36, s32[256]{0:T(256)S(1)} %iota.17), dimensions={0}, to_apply=%region_2.3 | sort | flops 2048 | bytes 4096 | tf_op jit(solution)/shard_map/jit(argsort)/sort | solution.py:78
  38.4 18.6 %all-gather.2.cloned.1.call-done = bf16[256,3584]{1,0:T(8,128)(2,1)} async-done(((bf16[64,3584]{1,0:T(8,128)(2,1)}), bf16[256,3584]{1,0:T(8,128)(2,1)}) %all-gather.2.cloned.1.call-update) | async-done | bytes 1835024 | tf_op jit(solution)/shard_map/all_gather | solution.py:72
  57.0 5.3 %gather_fusion = bf16[256,3584]{1,0:T(8,128)(2,1)S(1)} fusion(bf16[256,3584]{1,0:T(8,128)(2,1)} %all-gather.2.cloned.1.call-done, s32[1024]{0:T(1024)S(1)} %pad_clamp_fusion), kind=kCustom, calls=%fused_computation | custom fusion | bytes 3671040 | tf_op jit(solution)/shard_map/gather | solution.py:79
  62.3 26.8 %conditional.1 = (f32[256,3584]{1,0:T(8,128)}) conditional(s32[]{:T(128)} %convert_element_type.31, (bf16[256,3584]{1,0:T(8,128)(2,1)S(1)}, bf16[3584,2,2368]{0,2,1:T(8,128)(2,1)}, bf16[2368,3584]{1,0:T(8,128)(2,1)}) %tuple.11, (bf16[256,3584]{1,0:T(8,128)(2,1)S(1)}, bf16[3584,2,2368]{0,2,1:T(8,128)(2,1)}, bf16[2368,3584]{1,0:T(8,128)(2,1)}) %tuple.11), branch_computations={%region_4.5_spmd, %region_5.6_spmd} | conditional | flops 11409592320 | bytes 71221256 | solution.py:91
  62.5 15.5 %fusion.1 = f32[32,4736]{1,0:T(8,128)S(1)} fusion(bf16[3584,4736]{0,1:T(8,128)(2,1)} %bitcast.35, bf16[256,3584]{1,0:T(8,128)(2,1)S(1)} %get-tuple-element.20), kind=kOutput, calls=%fused_computation.4 | convolution fusion | flops 1086324736 | bytes 34783232 | tf_op jit(solution)/shard_map/cond/branch_0_fun/dot_general | solution.py:19
  78.0 8.9 %fusion.3 = f32[32,3584]{1,0:T(8,128)S(1)} fusion(bf16[2368,3584]{1,0:T(8,128)(2,1)} %get-tuple-element.22, f32[32,4736]{1,0:T(8,128)S(1)} %fusion.1), kind=kOutput, calls=%fused_computation.6 | convolution fusion | flops 543617024 | bytes 18055168 | tf_op jit(solution)/shard_map/cond/branch_0_fun/dot_general | solution.py:23
  86.9 2.3 %concatenate.4 = f32[256,3584]{1,0:T(8,128)} pad(f32[32,3584]{1,0:T(8,128)S(1)} %fusion.3, f32[]{:T(128)} %constant.17.clone), padding=0_224x0_0 | pad | bytes 4128772 | tf_op jit(solution)/shard_map/cond/branch_0_fun/concatenate | solution.py:85
  89.1 6.1 %scatter_custom_fusion = f32[256,3584]{1,0:T(8,128)} fusion(s32[256]{0:T(256)S(1)} %compare_select_fusion, f32[256,3584]{1,0:T(8,128)} %get-tuple-element.42, f32[]{:T(128)} %constant.12.clone.1), kind=kCustom, calls=%fused_computation.17 | custom fusion | bytes 3670528 | tf_op jit(solution)/shard_map/scatter | solution.py:92
  95.3 71.6 %reduce-scatter.2.cloned.1.call-done = f32[16,3584]{1,0:T(8,128)} async-done(((f32[256,3584]{1,0:T(8,128)}), f32[16,3584]{1,0:T(8,128)}) %reduce-scatter.2.cloned.1.call-update) | async-done | bytes 229392 | tf_op jit(solution)/shard_map/reduce_scatter | solution.py:93
  166.9 19.7 %all_gather.23 = f32[64,3584]{1,0:T(8,128)S(1)} all-gather(f32[16,3584]{1,0:T(8,128)} %reduce-scatter.2.cloned.1.call-done), channel_id=1, replica_groups=mesh['groups'=2,'seq'=4,'mp'=4] {'mp'}, dimensions={0}, use_global_device_ids=true | all-gather | bytes 1146880 | tf_op jit(solution)/shard_map/all_gather | solution.py:94
  186.5 0.8 fusion.24
  (18 shorter events, 0.1 us)
Async XLA Ops:
  6.5 17.0 %copy-start.3 = (u32[32]{0:T(128)S(1)}, u32[32]{0:T(128)}, u32[]{:S(2)}) copy-start(u32[32]{0:T(128)} %constant.50) | copy-start | bytes 388
  6.5 18.3 %copy-start.2 = (s32[64]{0:T(128)S(1)}, s32[64]{0:T(128)}, u32[]{:S(2)}) copy-start(s32[64]{0:T(128)} %param.16) | copy-start | bytes 772
  6.5 18.5 %copy-start.1 = (s32[64]{0:T(128)S(1)}, s32[64]{0:T(128)}, u32[]{:S(2)}) copy-start(s32[64]{0:T(128)} %param.15) | copy-start | bytes 772
  6.5 50.5 %all-gather.2.cloned.1.call-start = ((), (), s32[]{:S(2)}) async-start(), calls=%async_computation.1 | async-start | bytes 2293760 | tf_op jit(solution)/shard_map/all_gather | solution.py:72
  32.9 1.0 copy-start
  35.1 131.7 %reduce-scatter.2.cloned.1.call-start = ((), (), s32[]{:S(2)}) async-start(), calls=%async_computation.2 | async-start | bytes 3899392 | tf_op jit(solution)/shard_map/reduce_scatter | solution.py:93
Sparse Core Ops, SparseCore 0:
  35.3 21.7 all-gather.1
  95.4 71.4 reduce-scatter.1
where the time goes:
time: 195 us; the launch traced here: 194 us
  waiting for transfers between devices  90.2 us (46%)
  blocking collectives  38.1 us (20%)
  matrix products  26.1 us (13%)
  local copies, waits for them, and re-layouts  18.5 us (9%)
  between operations  14.2 us (7%)
  other arithmetic  6.91 us (4%)
    reduce_scatter x1, waiting for transfers between devices, body(): lax.psum_scatter(partial_value, ('seq', 'mp'), scatter_dimension=0, tiled...  71.6 us
    all_gather x1, blocking collectives, body(): ffn_sums = lax.all_gather(share, 'mp', axis=0, tiled=True)  19.7 us
    all_gather x1, waiting for transfers between devices, body(): lax.all_gather(normed, 'seq', axis=0, tiled=True)  18.6 us
    dot_general x1, matrix products, swiglu_block(): gate_up = jnp.dot(row_block, flat_in, preferred_element_type=jnp.float32)  15.5 us
    dot_general x1, matrix products, swiglu_block(): return jnp.dot(activated, out_block, preferred_element_type=jnp.float32)  8.86 us
    all_gather x1, blocking collectives, body(): key_piece = lax.all_gather(keys, 'seq', axis=0, tiled=True)  7.41 us
    scatter x1, local copies, waits for them, and re-layouts, body(): jnp.zeros((total_rows, D), jnp.float32).at[by_modality].set(sorted_out)  6.11 us
    all_gather x1, blocking collectives, body(): value_piece = lax.all_gather(values, 'seq', axis=0, tiled=True)  6.08 us
  transfers between devices with their start and end apart: 2, of which 2 were waited for; matrix products, arithmetic and copies ran while one was open for 2% of the time, Pallas kernels for 0%

commit v1 on v0

v1 whole, which is shorter than its diff:
```python
import functools
import math

import jax
import jax.numpy as jnp
from jax import lax
from jax.experimental import pallas as pl
from jax.experimental.pallas import tpu as pltpu
from jax.sharding import PartitionSpec as P

HEAD_SIZE = 128
FF = 18944
CHUNK = 16
NEG = -1e30


def reduce_kernel(
    seq_size, mp_size, part, resid, out,
    pair_recv, cross_send, cross_recv, own, right_send, right_recv, left_send, left_recv,
    pair_s, pair_r, cross_s, cross_r, right_s, right_r, left_s, left_r,
):
    chips = seq_size // 2
    rows = out.shape[0]
    chunks = rows // CHUNK
    me = lax.axis_index("seq")
    z = lax.axis_index("mp")
    core = lax.rem(me, 2)
    chip = lax.div(me, 2)
    partner = chip * 2 + (1 - core)

    def peer(d):
        return lax.rem(chip + d, chips) * 2 + core

    barrier = pltpu.get_barrier_semaphore()
    pl.semaphore_signal(barrier, inc=1, device_id={"seq": partner})
    for d in range(1, chips):
        pl.semaphore_signal(barrier, inc=1, device_id={"seq": peer(d)})

    @pl.when(z > 0)
    def _():
        pl.semaphore_signal(barrier, inc=1, device_id={"mp": z - 1})

    @pl.when(z < mp_size - 1)
    def _():
        pl.semaphore_signal(barrier, inc=1, device_id={"mp": z + 1})

    pl.semaphore_wait(
        barrier, chips + jnp.where(z > 0, 1, 0) + jnp.where(z < mp_size - 1, 1, 0)
    )

    def rows_of(k):
        return pl.ds(k * CHUNK, CHUNK)

    def block_of(seq_index, k):
        return pl.ds(pl.multiple_of(seq_index * rows + k * CHUNK, CHUNK), CHUNK)

    def pair_copy(d, k):
        return pltpu.make_async_remote_copy(
            src_ref=part.at[block_of(lax.rem(chip + d, chips) * 2 + (1 - core), k)],
            dst_ref=pair_recv.at[d, rows_of(k)],
            send_sem=pair_s.at[d, k], recv_sem=pair_r.at[d, k],
            device_id={"seq": partner},
        )

    def cross_copy(d, k):
        return pltpu.make_async_remote_copy(
            src_ref=cross_send.at[d - 1, rows_of(k)],
            dst_ref=cross_recv.at[d - 1, rows_of(k)],
            send_sem=cross_s.at[d - 1, k], recv_sem=cross_r.at[d - 1, k],
            device_id={"seq": peer(d)},
        )

    def right_copy(k):
        return pltpu.make_async_remote_copy(
            src_ref=right_send.at[rows_of(k)], dst_ref=right_recv.at[rows_of(k)],
            send_sem=right_s.at[k], recv_sem=right_r.at[k], device_id={"mp": z + 1},
        )

    def left_copy(k):
        return pltpu.make_async_remote_copy(
            src_ref=left_send.at[rows_of(k)], dst_ref=left_recv.at[rows_of(k)],
            send_sem=left_s.at[k], recv_sem=left_r.at[k], device_id={"mp": z - 1},
        )

    order = list(range(1, chips)) + [0]
    for k in range(chunks):
        for d in order:
            pair_copy(d, k).start()

    @pl.when(z == 0)
    def _():
        right_recv[...] = jnp.zeros_like(right_recv)

    @pl.when(z == mp_size - 1)
    def _():
        left_recv[...] = jnp.zeros_like(left_recv)

    f32 = jnp.float32
    for k in range(chunks):
        for d in range(1, chips):
            pair_copy(d, k).wait_recv()
            mine = part[block_of(peer(d), k), :].astype(f32)
            cross_send[d - 1, rows_of(k)] = (
                mine + pair_recv[d, rows_of(k)].astype(f32)
            ).astype(jnp.bfloat16)
            cross_copy(d, k).start()

    def gather_own(k):
        pair_copy(0, k).wait_recv()
        total = part[block_of(me, k), :].astype(f32) + pair_recv[0, rows_of(k)].astype(f32)
        for d in range(1, chips):
            cross_copy(d, k).wait_recv()
            total = total + cross_recv[d - 1, rows_of(k)].astype(f32)
        own[rows_of(k)] = total

    def step_right(k):
        @pl.when(z > 0)
        def _():
            right_copy(k).wait_recv()

        @pl.when(z < mp_size - 1)
        def _():
            right_send[rows_of(k)] = (
                own[rows_of(k)] + right_recv[rows_of(k)].astype(f32)
            ).astype(jnp.bfloat16)
            right_copy(k).start()

    def step_left(k):
        @pl.when(z < mp_size - 1)
        def _():
            left_copy(k).wait_recv()

        @pl.when(z > 0)
        def _():
            left_send[rows_of(k)] = (
                own[rows_of(k)] + left_recv[rows_of(k)].astype(f32)
            ).astype(jnp.bfloat16)
            left_copy(k).start()

    low_half = z * 2 < mp_size
    for t in range(chunks + 1):
        if t < chunks:
            gather_own(t)

        @pl.when(low_half)
        def _():
            if t < chunks:
                step_right(t)
            if t > 0:
                step_left(t - 1)

        @pl.when(jnp.logical_not(low_half))
        def _():
            if t < chunks:
                step_left(t)
            if t > 0:
                step_right(t - 1)

        if t > 0:
            here = rows_of(t - 1)
            ffn = own[here] + right_recv[here].astype(f32) + left_recv[here].astype(f32)
            out[here] = (resid[here].astype(f32) + ffn).astype(jnp.bfloat16)

    for k in range(chunks):
        for d in range(chips):
            pair_copy(d, k).wait_send()
        for d in range(1, chips):
            cross_copy(d, k).wait_send()

        @pl.when(z < mp_size - 1)
        def _():
            right_copy(k).wait_send()

        @pl.when(z > 0)
        def _():
            left_copy(k).wait_send()


def reduce_rows(part, residual, seq_size, mp_size):
    rows, width = residual.shape
    chips = seq_size // 2
    chunks = rows // CHUNK
    bf16 = jnp.bfloat16
    dma = pltpu.SemaphoreType.DMA
    crossing = max(chips - 1, 1)
    return pl.pallas_call(
        functools.partial(reduce_kernel, seq_size, mp_size),
        out_shape=jax.ShapeDtypeStruct((rows, width), bf16),
        in_specs=[pl.BlockSpec(memory_space=pltpu.VMEM)] * 2,
        out_specs=pl.BlockSpec(memory_space=pltpu.VMEM),
        scratch_shapes=[
            pltpu.VMEM((chips, rows, width), bf16),
            pltpu.VMEM((crossing, rows, width), bf16),
            pltpu.VMEM((crossing, rows, width), bf16),
            pltpu.VMEM((rows, width), jnp.float32),
            pltpu.VMEM((rows, width), bf16),
            pltpu.VMEM((rows, width), bf16),
            pltpu.VMEM((rows, width), bf16),
            pltpu.VMEM((rows, width), bf16),
            dma((chips, chunks)), dma((chips, chunks)),
            dma((crossing, chunks)), dma((crossing, chunks)),
            dma((chunks,)), dma((chunks,)), dma((chunks,)), dma((chunks,)),
        ],
        compiler_params=pltpu.CompilerParams(
            collective_id=1, has_side_effects=True, vmem_limit_bytes=40 * 1024 * 1024
        ),
        name="reduce_rows",
    )(part, residual)


def attend(queries, payload, all_payload, hidden_in, shard_index):
    row_count = queries.shape[0]
    kv_width = (payload.shape[1] - HEAD_SIZE) // 2
    group_count = kv_width // HEAD_SIZE
    head_count = queries.shape[1] // HEAD_SIZE
    total_rows = all_payload.shape[0]
    query_by_group = queries.reshape(
        row_count, group_count, head_count // group_count, HEAD_SIZE
    )
    key_by_group = all_payload[:, :kv_width].reshape(total_rows, group_count, HEAD_SIZE)
    value_by_group = all_payload[:, kv_width : 2 * kv_width].reshape(
        total_rows, group_count, HEAD_SIZE
    )
    scores = jnp.einsum(
        "rgqd,ngd->rgqn", query_by_group, key_by_group, preferred_element_type=jnp.float32
    ) * (1.0 / math.sqrt(HEAD_SIZE))
    position = shard_index * row_count + jnp.arange(row_count, dtype=jnp.int32)
    key_position = jnp.arange(total_rows, dtype=jnp.int32)
    own_doc = payload[:, 2 * kv_width]
    key_doc = all_payload[:, 2 * kv_width]
    visible = (own_doc[:, None] == key_doc[None, :]) & (
        key_position[None, :] <= position[:, None]
    )
    visible = visible[:, None, None, :]
    masked = jnp.where(visible, scores, NEG)
    row_max = jnp.max(masked, axis=-1)
    weights = jnp.where(visible, jnp.exp(masked - row_max[..., None]), 0.0)
    total = jnp.sum(weights, axis=-1)
    weighted = jnp.einsum(
        "rgqn,ngd->rgqd",
        weights.astype(jnp.bfloat16),
        value_by_group,
        preferred_element_type=jnp.float32,
    )
    attended = (weighted / total[..., None]).reshape(row_count, head_count * HEAD_SIZE)
    return (hidden_in.astype(jnp.float32) + attended).astype(jnp.bfloat16)


def normalise(residual, modality, norm_gains):
    wide = residual.astype(jnp.float32)
    mean_square = jnp.mean(wide * wide, axis=-1, keepdims=True)
    gain = jnp.where(modality[:, None] == 1, norm_gains[1][None, :], norm_gains[0][None, :])
    return (wide * lax.rsqrt(mean_square + 1e-06) * gain).astype(jnp.bfloat16)


def feed_forward(all_rows, wanted, input_weights, output_weights):
    unit_count = output_weights.shape[0]
    flat_in = input_weights.reshape(input_weights.shape[0], 2 * unit_count)
    gate_up = jnp.dot(all_rows, flat_in, preferred_element_type=jnp.float32)
    activated = jax.nn.silu(gate_up[:, :unit_count]) * gate_up[:, unit_count:]
    activated = jnp.where(wanted[:, None], activated, 0.0).astype(jnp.bfloat16)
    return jnp.dot(activated, output_weights, preferred_element_type=jnp.float32).astype(
        jnp.bfloat16
    )


def body(
    seq_size, mp_size,
    queries, keys, values, hidden_in, doc_ids, modality, input_weights, output_weights, norm_gains
):
    row_count = queries.shape[0]
    kv_width = keys.shape[1]
    shard_index = lax.axis_index("seq")
    device_index = shard_index * mp_size + lax.axis_index("mp")
    lane = jnp.arange(HEAD_SIZE, dtype=jnp.int32)[None, :]
    tags = jnp.where(lane == 0, doc_ids[:, None], jnp.where(lane == 1, modality[:, None], 0))
    payload = jnp.concatenate([keys, values, tags.astype(jnp.bfloat16)], axis=1)
    all_payload = lax.all_gather(payload, "seq", axis=0, tiled=True)
    residual = attend(queries, payload, all_payload, hidden_in, shard_index)
    normed = normalise(residual, modality, norm_gains)
    all_rows = lax.all_gather(normed, "seq", axis=0, tiled=True)
    is_image = device_index >= FF // output_weights.shape[0]
    wanted = (all_payload[:, 2 * kv_width + 1] > 0.5) == is_image
    part = feed_forward(all_rows, wanted, input_weights, output_weights)
    return reduce_rows(part, residual, seq_size, mp_size)


def solution(mesh):
    rows_spec = P(("groups", "seq"), None)
    in_specs = (
        rows_spec, rows_spec, rows_spec, rows_spec,
        P(("groups", "seq")), P(("groups", "seq")),
        P(None, None, ("seq", "mp")), P(("seq", "mp"), None), P(),
    )
    f = functools.partial(body, mesh.shape["seq"], mesh.shape["mp"])
    return jax.shard_map(f, mesh=mesh, in_specs=in_specs, out_specs=rows_spec, check_vma=False)
```

time: 195 us -> 124 us (0.64)
  waiting for transfers between devices: 90.2 us -> 22 us
  Pallas kernels: 0 us -> 38.5 us
  blocking collectives: 38.1 us -> 8.98 us
  local copies, waits for them, and re-layouts: 18.5 us -> 3.9 us
  matrix products: 26.1 us -> 32.8 us
  other arithmetic: 6.91 us -> 3.86 us
    reduce_scatter x1 -> x0, waiting for transfers between devices: 71.6 us -> none  [body(): lax.psum_scatter(partial_value, ('seq', 'mp'), scatter_dimension=0, tiled...]
    pallas_call x0 -> x1, Pallas kernels: none -> 38.5 us  [reduce_rows(): pl.pallas_call(functools.partial(reduce_kernel, seq_size, mp_size), out_s...]
    all_gather x3 -> x1, blocking collectives: 33.2 us -> 8.98 us  [body(): all_payload = lax.all_gather(payload, 'seq', axis=0, tiled=True)]
    scatter x1 -> x0, local copies, waits for them, and re-layouts: 6.11 us -> none  [body(): jnp.zeros((total_rows, D), jnp.float32).at[by_modality].set(sorted_out)]
    dot_general x4, matrix products: 26.1 us -> 31.9 us  [the longest x1 17.6 us: feed_forward(): gate_up = jnp.dot(all_rows, flat_in, preferred_element_type=jnp.float32)]
    gather x1 -> x0, local copies, waits for them, and re-layouts: 5.27 us -> none  [body(): sorted_rows = all_rows[by_modality]]
    unnamed x1 -> x0, blocking collectives: 4.94 us -> none
    all_gather x1, waiting for transfers between devices: 18.6 us -> 22 us  [body(): all_rows = lax.all_gather(normed, 'seq', axis=0, tiled=True)]
  transfers between devices with their start and end apart: 2 -> 1, of which waited for: 2 -> 1; matrix products, arithmetic and copies ran while one was open for 2% -> 0% of each run, Pallas kernels for 0% -> 0%
where the time goes in v1:
time: 124 us
  Pallas kernels  38.5 us (31%)
  matrix products  32.8 us (26%)
  waiting for transfers between devices  22 us (18%)
  between operations  13.6 us (11%)
  blocking collectives  8.98 us (7%)
  local copies, waits for them, and re-layouts  3.9 us (3%)
  other arithmetic  3.86 us (3%)
    pallas_call x1, Pallas kernels, reduce_rows(): pl.pallas_call(functools.partial(reduce_kernel, seq_size, mp_size), out_s...  38.5 us
    all_gather x1, waiting for transfers between devices, body(): all_rows = lax.all_gather(normed, 'seq', axis=0, tiled=True)  22 us
    dot_general x1, matrix products, feed_forward(): gate_up = jnp.dot(all_rows, flat_in, preferred_element_type=jnp.float32)  17.6 us
    dot_general x1, matrix products, feed_forward(): jnp.dot(activated, output_weights, preferred_element_type=jnp.float32)  12.4 us
    all_gather x1, blocking collectives, body(): all_payload = lax.all_gather(payload, 'seq', axis=0, tiled=True)  8.98 us
  transfers between devices with their start and end apart: 1, of which 1 were waited for; matrix products, arithmetic and copies ran while one was open for 0% of the time, Pallas kernels for 0%

profile of v1, /device:TPU:0, one launch (start us, length us, event | category | flops | bytes accessed | tf_op | source)
XLA Modules:
  0.0 123.6 jit_solution(16261023689072246325)
XLA Ops:
  6.5 0.0 copy-start.2
  6.5 0.0 copy-start
  6.5 0.0 all-gather.2.cloned.1.call-start
  6.5 0.7 broadcast_compare_fusion
  7.3 0.7 select_convert_fusion
  8.0 0.1 slice_reduce_fusion.1
  8.1 0.9 pad_maximum_fusion
  9.0 9.0 %all_gather.6 = bf16[256,1152]{1,0:T(8,128)(2,1)S(1)} all-gather(bf16[64,1152]{1,0:T(8,128)(2,1)S(1)} %pad_maximum_fusion), channel_id=1, replica_groups=mesh['groups'=2,'seq'=4,'mp'=4] {'seq'}, dimensions={0}, use_global_device_ids=true | all-gather | bytes 737280 | tf_op jit(solution)/shard_map/all_gather | solution.py:278
  18.0 0.1 slice_reduce_fusion
  18.2 0.0 copy-done.2
  18.2 0.1 slice_reduce_fusion.3
  18.3 0.1 copy.31
  18.4 0.1 copy.30
  18.5 0.0 copy-done
  18.6 0.6 reshape.90
  19.1 0.4 fusion.16
  19.5 0.1 fusion.22
  19.6 0.9 fusion.34
  20.5 1.6 %fusion.4 = f32[64,4,7,128]{3,0,2,1:T(8,128)} fusion(bf16[256,4,128,1]{0,2,3,1:T(8,128)(2,1)S(1)} %bitcast.34, f32[64,4,7]{0,2,1:T(8,128)S(1)} %fusion.34, f32[4,256,64,7]{1,2,3,0:T(8,128)S(1)} %fusion.16, pred[64,256]{1,0:T(8,128)(4,1)S(1)} %fusion.22), kind=kOutput, calls=%fused_computation.9 | convolution fusion | flops 119965696 | bytes 3038208 | tf_op jit(solution)/shard_map/rgqn,ngd->rgqd/dot_general | solution.py:239
  22.1 0.0 copy-start.1
  22.1 1.8 %copy.23 = f32[64,4,7,128]{3,2,1,0:T(8,128)S(1)} copy(f32[64,4,7,128]{3,0,2,1:T(8,128)} %fusion.4) | data formatting | bytes 1835008 | tf_op jit(solution)/shard_map/div | solution.py:245
  23.9 0.2 reshape.91
  24.1 0.0 copy-done.1
  24.1 0.2 fusion.9
  24.4 1.0 fusion.11
  25.4 0.0 all-gather.2.cloned.1.call-update
  25.4 0.2 compare_reduce_fusion
  25.6 22.0 %all-gather.2.cloned.1.call-done = bf16[256,3584]{1,0:T(8,128)(2,1)} async-done(((bf16[64,3584]{1,0:T(8,128)(2,1)}), bf16[256,3584]{1,0:T(8,128)(2,1)}) %all-gather.2.cloned.1.call-update) | async-done | bytes 1835024 | tf_op jit(solution)/shard_map/all_gather | solution.py:281
  47.5 17.6 %fusion.37 = f32[256,4736]{1,0:T(8,128)} fusion(bf16[256,3584]{1,0:T(8,128)(2,1)} %all-gather.2.cloned.1.call-done, bf16[3584,4736]{0,1:T(8,128)(2,1)} %bitcast.35), kind=kOutput, calls=%fused_computation.49 | convolution fusion | flops 8690597888 | bytes 40632320 | tf_op jit(solution)/shard_map/dot_general | solution.py:259
  65.1 12.4 %convolution_convert_fusion.part = bf16[256,3584]{1,0:T(8,128)(2,1)S(1)} fusion(bf16[2368,3584]{1,0:T(8,128)(2,1)} %param.16, f32[256,4736]{1,0:T(8,128)} %fusion.37, pred[256]{0:T(512)(128)(4,1)S(1)} %compare_reduce_fusion), kind=kOutput, calls=%fused_computation.1 | convolution fusion | flops 4350459904 | bytes 23789824 | tf_op jit(solution)/shard_map/dot_general | solution.py:262
  77.5 38.5 %reduce_rows.1 = bf16[64,3584]{1,0:T(8,128)(2,1)S(1)} custom-call(bf16[256,3584]{1,0:T(8,128)(2,1)S(1)} %convolution_convert_fusion.part, bf16[64,3584]{1,0:T(8,128)(2,1)S(1)} %get-tuple-element.8.resid), custom_call_target="tpu_custom_call" | custom-call | tf_op jit(solution)/shard_map/reduce_rows/pallas_call | solution.py:186
  116.0 0.8 copy.41
  (4 shorter events, 0.1 us)
Async XLA Ops:
  6.5 11.6 %copy-start.2 = (f32[2,3584]{1,0:T(2,128)S(1)}, f32[2,3584]{1,0:T(2,128)}, u32[]{:S(2)}) copy-start(f32[2,3584]{1,0:T(2,128)} %param.17) | copy-start | bytes 86020
  6.5 12.0 %copy-start = (bf16[64,3584]{1,0:T(8,128)(2,1)S(1)}, bf16[64,3584]{1,0:T(8,128)(2,1)}, u32[]{:S(2)}) copy-start(bf16[64,3584]{1,0:T(8,128)(2,1)} %param.9) | copy-start | bytes 1376260
  6.5 41.0 %all-gather.2.cloned.1.call-start = ((), (), s32[]{:S(2)}) async-start(), calls=%async_computation | async-start | bytes 2293760 | tf_op jit(solution)/shard_map/all_gather | solution.py:281
  22.1 2.0 %copy-start.1 = (bf16[64,3584]{1,0:T(8,128)(2,1)S(1)}, bf16[64,3584]{1,0:T(8,128)(2,1)}, u32[]{:S(2)}) copy-start(bf16[64,3584]{1,0:T(8,128)(2,1)} %param.12) | copy-start | bytes 1376260
Sparse Core Ops, SparseCore 0:
  25.5 21.9 all-gather.1

commit v2 on v1

v2 whole, which is shorter than its diff:
```python
import functools
import math

import jax
import jax.numpy as jnp
from jax import lax
from jax.experimental import pallas as pl
from jax.experimental.pallas import tpu as pltpu
from jax.sharding import PartitionSpec as P

HEAD_SIZE = 128
FF = 18944
CHUNK = 16
COLS = 512
UNIT_TILE = 256
ROW_TILE = 256
SLOTS = 6
LAG = 2
NEG = -1e30


def split_units(units):
    if units % 16:
        return [(0, units)]
    return [(o, min(UNIT_TILE, units - o)) for o in range(0, units, UNIT_TILE)]


def ffn_kernel(
    seq_size, mp_size, normed, resid, wanted, w_in, w_out, out,
    x, ring, w_down, act, part,
    pair_recv, cross_send, cross_recv, own, right_send, right_recv, left_send, left_recv,
    near_s, near_r, far_s, far_r, relay_s, relay_r, keep_sem, ring_sem, down_sem,
    pair_s, pair_r, cross_s, cross_r, right_s, right_r, left_s, left_r,
):
    chips = seq_size // 2
    rows, width = out.shape
    chunks = width // COLS
    total_rows = x.shape[0]
    units = w_down.shape[0]
    tiles = split_units(units)
    slots = ring.shape[0]
    f32 = jnp.float32
    me = lax.axis_index("seq")
    z = lax.axis_index("mp")
    core = lax.rem(me, 2)
    chip = lax.div(me, 2)
    partner = chip * 2 + (1 - core)

    def peer(d):
        return lax.rem(chip + d, chips) * 2 + core

    def source(d):
        return lax.rem(chip + chips - d, chips) * 2 + core

    def load(t):
        offset, size = tiles[t]
        return pltpu.make_async_copy(
            w_in.at[:, pl.ds(offset, size)],
            ring.at[t % slots, :, pl.ds(0, size)],
            ring_sem.at[t],
        )

    down_load = pltpu.make_async_copy(w_out, w_down, down_sem)
    for t in range(min(slots, len(tiles))):
        load(t).start()
    down_load.start()

    barrier = pltpu.get_barrier_semaphore()
    pl.semaphore_signal(barrier, inc=1, device_id={"seq": partner})
    for d in range(1, chips):
        pl.semaphore_signal(barrier, inc=1, device_id={"seq": peer(d)})

    @pl.when(z > 0)
    def _():
        pl.semaphore_signal(barrier, inc=1, device_id={"mp": z - 1})

    @pl.when(z < mp_size - 1)
    def _():
        pl.semaphore_signal(barrier, inc=1, device_id={"mp": z + 1})

    pl.semaphore_wait(
        barrier, chips + jnp.where(z > 0, 1, 0) + jnp.where(z < mp_size - 1, 1, 0)
    )

    row_chunks = rows // CHUNK

    def place(seq_index, k):
        return x.at[pl.ds(pl.multiple_of(seq_index * rows + k * CHUNK, CHUNK), CHUNK)]

    def near_copy(k):
        return pltpu.make_async_remote_copy(
            src_ref=normed.at[pl.ds(k * CHUNK, CHUNK)], dst_ref=place(me, k),
            send_sem=near_s.at[k], recv_sem=near_r.at[k], device_id={"seq": partner},
        )

    def far_copy(d, k):
        return pltpu.make_async_remote_copy(
            src_ref=normed.at[pl.ds(k * CHUNK, CHUNK)], dst_ref=place(me, k),
            send_sem=far_s.at[d - 1, k], recv_sem=far_r.at[d - 1, k],
            device_id={"seq": peer(d)},
        )

    def relay_copy(d, k):
        return pltpu.make_async_remote_copy(
            src_ref=place(source(d), k), dst_ref=place(source(d), k),
            send_sem=relay_s.at[d - 1, k], recv_sem=relay_r.at[d - 1, k],
            device_id={"seq": partner},
        )

    keep = pltpu.make_async_copy(
        normed, x.at[pl.ds(pl.multiple_of(me * rows, rows), rows)], keep_sem
    )
    for k in range(row_chunks):
        for d in range(1, chips):
            far_copy(d, k).start()
    for k in range(row_chunks):
        near_copy(k).start()
    keep.start()

    @pl.when(z == 0)
    def _():
        right_recv[...] = jnp.zeros_like(right_recv)

    @pl.when(z == mp_size - 1)
    def _():
        left_recv[...] = jnp.zeros_like(left_recv)

    for k in range(row_chunks):
        for d in range(1, chips):
            far_copy(d, k).wait_recv()
            relay_copy(d, k).start()
    keep.wait()
    for k in range(row_chunks):
        near_copy(k).wait()
        for d in range(1, chips):
            far_copy(d, k).wait_send()
            relay_copy(d, k).wait()

    blocks = total_rows // ROW_TILE if total_rows % ROW_TILE == 0 else 1
    block_rows = total_rows // blocks
    last_dims = (((1,), (1,)), ((), ()))

    def rows_at(i):
        return pl.ds(pl.multiple_of(i * block_rows, block_rows), block_rows)

    for t, (offset, size) in enumerate(tiles):
        load(t).wait()
        slot = t % slots

        def gate_up(i, carry, slot=slot, offset=offset, size=size):
            here = x[rows_at(i), :]
            gate = lax.dot_general(
                here, ring[slot, 0, :size, :], last_dims, preferred_element_type=f32
            )
            up = lax.dot_general(
                here, ring[slot, 1, :size, :], last_dims, preferred_element_type=f32
            )
            value = gate / (1.0 + jnp.exp(-gate)) * up
            value = jnp.where(wanted[rows_at(i), :1] > 0.5, value, 0.0)
            act[rows_at(i), pl.ds(offset, size)] = value.astype(jnp.bfloat16)
            return carry

        lax.fori_loop(0, blocks, gate_up, 0)
        if t + slots < len(tiles):
            load(t + slots).start()
    down_load.wait()

    def cols(k):
        return pl.ds(k * COLS, COLS)

    def block_of(seq_index):
        return pl.ds(pl.multiple_of(seq_index * rows, rows), rows)

    def pair_copy(d, k):
        return pltpu.make_async_remote_copy(
            src_ref=part.at[k, block_of(lax.rem(chip + d, chips) * 2 + (1 - core))],
            dst_ref=pair_recv.at[k, d],
            send_sem=pair_s.at[d, k], recv_sem=pair_r.at[d, k],
            device_id={"seq": partner},
        )

    def cross_copy(d, k):
        return pltpu.make_async_remote_copy(
            src_ref=cross_send.at[k, d - 1], dst_ref=cross_recv.at[k, d - 1],
            send_sem=cross_s.at[d - 1, k], recv_sem=cross_r.at[d - 1, k],
            device_id={"seq": peer(d)},
        )

    def right_copy(k):
        return pltpu.make_async_remote_copy(
            src_ref=right_send.at[k], dst_ref=right_recv.at[k],
            send_sem=right_s.at[k], recv_sem=right_r.at[k], device_id={"mp": z + 1},
        )

    def left_copy(k):
        return pltpu.make_async_remote_copy(
            src_ref=left_send.at[k], dst_ref=left_recv.at[k],
            send_sem=left_s.at[k], recv_sem=left_r.at[k], device_id={"mp": z - 1},
        )

    def cross_stage(k):
        for d in range(1, chips):
            pair_copy(d, k).wait_recv()
            cross_send[k, d - 1] = (
                part[k, block_of(peer(d)), :].astype(f32) + pair_recv[k, d].astype(f32)
            ).astype(jnp.bfloat16)
            cross_copy(d, k).start()

    order = list(range(1, chips)) + [0]
    for k in range(chunks):

        def down(i, carry, k=k):
            part[k, rows_at(i), :] = jnp.dot(
                act[rows_at(i), :], w_down[:, cols(k)], preferred_element_type=f32
            ).astype(jnp.bfloat16)
            return carry

        lax.fori_loop(0, blocks, down, 0)
        for d in order:
            pair_copy(d, k).start()
        if k > 0:
            cross_stage(k - 1)
    cross_stage(chunks - 1)

    def gather_own(k):
        pair_copy(0, k).wait_recv()
        total = part[k, block_of(me), :].astype(f32) + pair_recv[k, 0].astype(f32)
        for d in range(1, chips):
            cross_copy(d, k).wait_recv()
            total = total + cross_recv[k, d - 1].astype(f32)
        own[k] = total

    def step_right(k):
        @pl.when(z > 0)
        def _():
            right_copy(k).wait_recv()

        @pl.when(z < mp_size - 1)
        def _():
            right_send[k] = (own[k] + right_recv[k].astype(f32)).astype(jnp.bfloat16)
            right_copy(k).start()

    def step_left(k):
        @pl.when(z < mp_size - 1)
        def _():
            left_copy(k).wait_recv()

        @pl.when(z > 0)
        def _():
            left_send[k] = (own[k] + left_recv[k].astype(f32)).astype(jnp.bfloat16)
            left_copy(k).start()

    low_half = z * 2 < mp_size
    for t in range(chunks + LAG):
        if t < chunks:
            gather_own(t)

        @pl.when(low_half)
        def _():
            if t < chunks:
                step_right(t)
            if t >= LAG:
                step_left(t - LAG)

        @pl.when(jnp.logical_not(low_half))
        def _():
            if t < chunks:
                step_left(t)
            if t >= LAG:
                step_right(t - LAG)

        if t >= LAG:
            k = t - LAG
            ffn = own[k] + right_recv[k].astype(f32) + left_recv[k].astype(f32)
            out[:, cols(k)] = (resid[:, cols(k)].astype(f32) + ffn).astype(jnp.bfloat16)

    for k in range(chunks):
        for d in range(chips):
            pair_copy(d, k).wait_send()
        for d in range(1, chips):
            cross_copy(d, k).wait_send()

        @pl.when(z < mp_size - 1)
        def _():
            right_copy(k).wait_send()

        @pl.when(z > 0)
        def _():
            left_copy(k).wait_send()


def feed_forward(normed, residual, wanted, input_weights, output_weights, seq_size, mp_size):
    rows, width = residual.shape
    total_rows = rows * seq_size
    units = output_weights.shape[0]
    chips = seq_size // 2
    chunks = width // COLS
    row_chunks = rows // CHUNK
    bf16 = jnp.bfloat16
    dma = pltpu.SemaphoreType.DMA
    crossing = max(chips - 1, 1)
    tiles = split_units(units)
    slots = min(SLOTS, len(tiles))
    flops = 6 * total_rows * width * units
    vmem = pl.BlockSpec(memory_space=pltpu.VMEM)
    hbm = pl.BlockSpec(memory_space=pl.ANY)
    return pl.pallas_call(
        functools.partial(ffn_kernel, seq_size, mp_size),
        out_shape=jax.ShapeDtypeStruct((rows, width), bf16),
        in_specs=[vmem, vmem, vmem, hbm, hbm],
        out_specs=vmem,
        scratch_shapes=[
            pltpu.VMEM((total_rows, width), bf16),
            pltpu.VMEM((slots, 2, tiles[0][1], width), bf16),
            pltpu.VMEM((units, width), bf16),
            pltpu.VMEM((total_rows, units), bf16),
            pltpu.VMEM((chunks, total_rows, COLS), bf16),
            pltpu.VMEM((chunks, chips, rows, COLS), bf16),
            pltpu.VMEM((chunks, crossing, rows, COLS), bf16),
            pltpu.VMEM((chunks, crossing, rows, COLS), bf16),
            pltpu.VMEM((chunks, rows, COLS), jnp.float32),
            pltpu.VMEM((chunks, rows, COLS), bf16),
            pltpu.VMEM((chunks, rows, COLS), bf16),
            pltpu.VMEM((chunks, rows, COLS), bf16),
            pltpu.VMEM((chunks, rows, COLS), bf16),
            dma((row_chunks,)), dma((row_chunks,)),
            dma((crossing, row_chunks)), dma((crossing, row_chunks)),
            dma((crossing, row_chunks)), dma((crossing, row_chunks)),
            dma(()), dma((len(tiles),)), dma(()),
            dma((chips, chunks)), dma((chips, chunks)),
            dma((crossing, chunks)), dma((crossing, chunks)),
            dma((chunks,)), dma((chunks,)), dma((chunks,)), dma((chunks,)),
        ],
        compiler_params=pltpu.CompilerParams(
            collective_id=1, has_side_effects=True, vmem_limit_bytes=58 * 1024 * 1024
        ),
        cost_estimate=pl.CostEstimate(
            flops=flops, bytes_accessed=6 * units * width, transcendentals=0
        ),
        name="feed_forward",
    )(normed, residual, wanted, input_weights, output_weights)


def attend(queries, payload, all_payload, hidden_in, shard_index):
    row_count = queries.shape[0]
    kv_width = (payload.shape[1] - HEAD_SIZE) // 2
    group_count = kv_width // HEAD_SIZE
    head_count = queries.shape[1] // HEAD_SIZE
    total_rows = all_payload.shape[0]
    query_by_group = queries.reshape(
        row_count, group_count, head_count // group_count, HEAD_SIZE
    )
    key_by_group = all_payload[:, :kv_width].reshape(total_rows, group_count, HEAD_SIZE)
    value_by_group = all_payload[:, kv_width : 2 * kv_width].reshape(
        total_rows, group_count, HEAD_SIZE
    )
    scores = jnp.einsum(
        "rgqd,ngd->rgqn", query_by_group, key_by_group, preferred_element_type=jnp.float32
    ) * (1.0 / math.sqrt(HEAD_SIZE))
    position = shard_index * row_count + jnp.arange(row_count, dtype=jnp.int32)
    key_position = jnp.arange(total_rows, dtype=jnp.int32)
    own_doc = payload[:, 2 * kv_width]
    key_doc = all_payload[:, 2 * kv_width]
    visible = (own_doc[:, None] == key_doc[None, :]) & (
        key_position[None, :] <= position[:, None]
    )
    visible = visible[:, None, None, :]
    masked = jnp.where(visible, scores, NEG)
    row_max = jnp.max(masked, axis=-1)
    weights = jnp.where(visible, jnp.exp(masked - row_max[..., None]), 0.0)
    total = jnp.sum(weights, axis=-1)
    weighted = jnp.einsum(
        "rgqn,ngd->rgqd",
        weights.astype(jnp.bfloat16),
        value_by_group,
        preferred_element_type=jnp.float32,
    )
    attended = (weighted / total[..., None]).reshape(row_count, head_count * HEAD_SIZE)
    return (hidden_in.astype(jnp.float32) + attended).astype(jnp.bfloat16)


def normalise(residual, modality, norm_gains):
    wide = residual.astype(jnp.float32)
    mean_square = jnp.mean(wide * wide, axis=-1, keepdims=True)
    gain = jnp.where(modality[:, None] == 1, norm_gains[1][None, :], norm_gains[0][None, :])
    return (wide * lax.rsqrt(mean_square + 1e-06) * gain).astype(jnp.bfloat16)


def body(
    seq_size, mp_size,
    queries, keys, values, hidden_in, doc_ids, modality, input_weights, output_weights, norm_gains
):
    row_count = queries.shape[0]
    kv_width = keys.shape[1]
    shard_index = lax.axis_index("seq")
    device_index = shard_index * mp_size + lax.axis_index("mp")
    lane = jnp.arange(HEAD_SIZE, dtype=jnp.int32)[None, :]
    tags = jnp.where(lane == 0, doc_ids[:, None], jnp.where(lane == 1, modality[:, None], 0))
    payload = jnp.concatenate([keys, values, tags.astype(jnp.bfloat16)], axis=1)
    all_payload = lax.all_gather(payload, "seq", axis=0, tiled=True)
    residual = attend(queries, payload, all_payload, hidden_in, shard_index)
    normed = normalise(residual, modality, norm_gains)
    is_image = device_index >= FF // output_weights.shape[0]
    wanted = (all_payload[:, 2 * kv_width + 1] > 0.5) == is_image
    wanted = jnp.broadcast_to(wanted[:, None], (wanted.shape[0], HEAD_SIZE)).astype(jnp.float32)
    by_unit = jnp.transpose(input_weights, (1, 2, 0))
    return feed_forward(
        normed, residual, wanted, by_unit, output_weights, seq_size, mp_size
    )


def solution(mesh):
    rows_spec = P(("groups", "seq"), None)
    in_specs = (
        rows_spec, rows_spec, rows_spec, rows_spec,
        P(("groups", "seq")), P(("groups", "seq")),
        P(None, None, ("seq", "mp")), P(("seq", "mp"), None), P(),
    )
    f = functools.partial(body, mesh.shape["seq"], mesh.shape["mp"])
    return jax.shard_map(f, mesh=mesh, in_specs=in_specs, out_specs=rows_spec, check_vma=False)
```

time: 124 us -> 103 us (0.83)
  Pallas kernels: 38.5 us -> 78.7 us
  matrix products: 32.8 us -> 3.43 us
  waiting for transfers between devices: 22 us -> 0 us
  between operations: 13.6 us -> 0.17 us
  local copies, waits for them, and re-layouts: 3.9 us -> 6.74 us
    pallas_call x1, Pallas kernels: 38.5 us -> 78.7 us  [feed_forward(): pl.pallas_call(functools.partial(ffn_kernel, seq_size, mp_size), out_shap...]
    dot_general x2 -> x0, matrix products: 29.9 us -> none  [the longest x1 17.6 us: feed_forward(): gate_up = jnp.dot(all_rows, flat_in, preferred_element_type=jnp.float32)]
    all_gather x1 -> x0, waiting for transfers between devices: 22 us -> none  [body(): all_rows = lax.all_gather(normed, 'seq', axis=0, tiled=True)]
    unnamed x9 -> x15, local copies, waits for them, and re-layouts: 1.05 us -> 2.9 us
    slice x1, local copies, waits for them, and re-layouts: 0.07 us -> 1.51 us  [normalise(): norm_gains[1][None, :]]
  transfers between devices with their start and end apart: 1 -> 0, of which waited for: 1 -> 0; matrix products, arithmetic and copies ran while one was open for 0% -> 0% of each run, Pallas kernels for 0% -> 0%
where the time goes in v2:
time: 103 us; the launch traced here: 102 us
  Pallas kernels  78.7 us (76%)
  blocking collectives  8.98 us (9%)
  local copies, waits for them, and re-layouts  6.74 us (7%)
  other arithmetic  4.36 us (4%)
  matrix products  3.43 us (3%)
    pallas_call x1, Pallas kernels, feed_forward(): pl.pallas_call(functools.partial(ffn_kernel, seq_size, mp_size), out_shap...  78.7 us
    all_gather x1, blocking collectives, body(): all_payload = lax.all_gather(payload, 'seq', axis=0, tiled=True)  8.98 us
    unnamed x15, local copies, waits for them, and re-layouts  2.9 us

profile of v2, /device:TPU:0, one launch (start us, length us, event | category | flops | bytes accessed | tf_op | source)
XLA Modules:
  0.0 102.4 jit_solution(15371186560189281613)
XLA Ops:
  0.0 1.2 %broadcast_compare_fusion = pred[64]{0:T(512)(128)(4,1)} fusion(s32[64]{0:T(128)} %param.14), kind=kLoop, calls=%fused_computation.32 | loop fusion | flops 64 | bytes 320 | tf_op jit(solution)/shard_map/eq | solution.py:385
  1.3 0.7 select_convert_fusion
  2.0 0.1 slice_reduce_fusion.1
  2.1 1.5 %slice_reduce_fusion.3 = (f32[3584]{0:T(1024)S(1)}, f32[3584]{0:T(1024)}) fusion(f32[2,3584]{1,0:T(2,128)} %param.17), kind=kLoop, calls=%fused_computation.26 | loop fusion | bytes 57344 | tf_op jit(solution)/shard_map/slice | solution.py:385
  3.6 0.9 pad_maximum_fusion
  4.5 9.0 %all_gather.3 = bf16[256,1152]{1,0:T(8,128)(2,1)S(1)} all-gather(bf16[64,1152]{1,0:T(8,128)(2,1)S(1)} %pad_maximum_fusion), channel_id=1, replica_groups=mesh['groups'=2,'seq'=4,'mp'=4] {'seq'}, dimensions={0}, use_global_device_ids=true | all-gather | bytes 737280 | tf_op jit(solution)/shard_map/all_gather | solution.py:400
  13.5 0.2 convert_reduce_fusion
  13.7 0.1 slice_reduce_fusion
  13.8 0.1 copy.31
  14.0 0.1 fusion.16
  14.1 0.0 copy-start.4
  14.1 0.8 broadcast_in_dim.111.wanted
  14.9 0.1 copy.30
  15.0 0.0 copy-done.1
  15.0 0.6 reshape.89
  15.6 1.5 %fusion.26 = f32[64,4,7]{0,2,1:T(8,128)} fusion(pred[64,256]{1,0:T(8,128)(4,1)S(1)} %fusion.16, bf16[256,4,128,1]{0,2,3,1:T(8,128)(2,1)S(1)} %bitcast.30, bf16[64,4,7,128]{3,2,1,0:T(8,128)(2,1)S(1)} %reshape.89), kind=kOutput, calls=%fused_computation.39 | convolution fusion | flops 119734528 | bytes 744448 | tf_op jit(solution)/shard_map/sub | solution.py:370
  17.1 0.0 copy-done.4
  17.1 0.4 fusion.10
  17.5 1.6 %fusion.2 = f32[64,4,7,128]{3,0,2,1:T(8,128)S(1)} fusion(bf16[256,4,128,1]{0,2,3,1:T(8,128)(2,1)S(1)} %bitcast.32, f32[64,4,7]{0,2,1:T(8,128)} %fusion.26, f32[4,256,64,7]{1,2,3,0:T(8,128)S(1)} %fusion.10, pred[64,256]{1,0:T(8,128)(4,1)} %copy-done.4), kind=kOutput, calls=%fused_computation.5 | convolution fusion | flops 119965696 | bytes 3038208 | tf_op jit(solution)/shard_map/rgqn,ngd->rgqd/dot_general | solution.py:372
  19.0 0.5 copy.23
  19.6 0.0 copy-start.2
  19.6 0.0 copy-start.3
  19.6 0.0 copy-start.5
  19.6 0.2 reshape.90
  19.8 0.8 copy-done.2
  20.6 0.2 fusion.3
  20.8 0.0 copy-start
  20.9 0.0 copy-done.3
  20.9 1.0 fusion.5.normed
  21.9 0.0 copy-done
  21.9 78.7 %feed_forward.1 = bf16[64,3584]{1,0:T(8,128)(2,1)} custom-call(bf16[64,3584]{1,0:T(8,128)(2,1)} %fusion.5.normed, bf16[64,3584]{1,0:T(8,128)(2,1)} %copy-done, f32[256,128]{1,0:T(8,128)} %broadcast_in_dim.111.wanted, bf16[2,2368,3584]{2,1,0:T(8,128)(2,1)} %bitcast.29, bf16[2368,3584]{1,0:T(8,128)(2,1)} %w_out.1), custom_call_target="tpu_custom_call" | custom-call | flops 13035896832 | bytes 50921472 | tf_op jit(solution)/shard_map/feed_forward/pallas_call | solution.py:307
  100.6 1.8 %copy.41 = bf16[64,3584]{1,0:T(8,128)(2,1)} copy(bf16[64,3584]{1,0:T(8,128)(2,1)} %feed_forward.1) | data formatting | bytes 917504
  (6 shorter events, 0.1 us)
Async XLA Ops:
  0.0 15.0 %copy-start.1 = (bf16[64,3584]{1,0:T(8,128)(2,1)S(1)}, bf16[64,3584]{1,0:T(8,128)(2,1)}, u32[]{:S(2)}) copy-start(bf16[64,3584]{1,0:T(8,128)(2,1)} %param.9) | copy-start | bytes 1376260
  14.1 3.0 %copy-start.4 = (pred[64,256]{1,0:T(8,128)(4,1)}, pred[64,256]{1,0:T(8,128)(4,1)S(1)}, u32[]{:S(2)}) copy-start(pred[64,256]{1,0:T(8,128)(4,1)S(1)} %fusion.16) | copy-start | bytes 49156
  19.6 1.0 copy-start.2
  19.6 1.3 %copy-start.3 = (f32[3584]{0:T(1024)S(1)}, f32[3584]{0:T(1024)}, u32[]{:S(2)}) copy-start(f32[3584]{0:T(1024)} %get-tuple-element.6) | copy-start | bytes 43012
  19.6 1.3 %copy-start.5 = (pred[64]{0:T(512)(128)(4,1)S(1)}, pred[64]{0:T(512)(128)(4,1)}, u32[]{:S(2)}) copy-start(pred[64]{0:T(512)(128)(4,1)} %broadcast_compare_fusion) | copy-start | bytes 196
  20.8 1.0 copy-start

commit v3 on v2

--- a/solution.py
+++ b/solution.py
@@ -26,7 +26,8 @@
 
 
 def ffn_kernel(
-    seq_size, mp_size, normed, resid, wanted, w_in, w_out, out,
+    seq_size, mp_size, queries, keys, values, tags, hidden, gains, w_in, w_out, out,
+    kv, resid, normed, kv_s, kv_r,
     x, ring, w_down, act, part,
     pair_recv, cross_send, cross_recv, own, right_send, right_recv, left_send, left_recv,
     near_s, near_r, far_s, far_r, relay_s, relay_r, keep_sem, ring_sem, down_sem,
@@ -66,9 +67,8 @@
     down_load.start()
 
     barrier = pltpu.get_barrier_semaphore()
-    pl.semaphore_signal(barrier, inc=1, device_id={"seq": partner})
-    for d in range(1, chips):
-        pl.semaphore_signal(barrier, inc=1, device_id={"seq": peer(d)})
+    for d in range(1, seq_size):
+        pl.semaphore_signal(barrier, inc=1, device_id={"seq": lax.rem(me + d, seq_size)})
 
     @pl.when(z > 0)
     def _():
@@ -79,9 +79,80 @@
         pl.semaphore_signal(barrier, inc=1, device_id={"mp": z + 1})
 
     pl.semaphore_wait(
-        barrier, chips + jnp.where(z > 0, 1, 0) + jnp.where(z < mp_size - 1, 1, 0)
+        barrier, seq_size - 1 + jnp.where(z > 0, 1, 0) + jnp.where(z < mp_size - 1, 1, 0)
     )
 
+    kv_width = keys.shape[1]
+    group_count = kv_width // HEAD_SIZE
+    heads = width // HEAD_SIZE // group_count
+    own_rows = pl.ds(pl.multiple_of(me * rows, rows), rows)
+    pieces = ((keys, 0, kv_width), (values, kv_width, kv_width), (tags, 2 * kv_width, HEAD_SIZE))
+
+    def kv_copy(d, p):
+        ref, offset, size = pieces[p]
+        return pltpu.make_async_remote_copy(
+            src_ref=ref, dst_ref=kv.at[own_rows, pl.ds(offset, size)],
+            send_sem=kv_s.at[d - 1, p], recv_sem=kv_r.at[d - 1, p],
+            device_id={"seq": lax.rem(me + d, seq_size)},
+        )
+
+    for d in range(1, seq_size):
+        for p in range(3):
+            kv_copy(d, p).start()
+    for ref, offset, size in pieces:
+        kv[own_rows, pl.ds(offset, size)] = ref[...]
+    for d in range(1, seq_size):
+        for p in range(3):
+            kv_copy(d, p).wait()
+
+    lane = lax.broadcasted_iota(jnp.int32, (rows, HEAD_SIZE), 1)
+    own_tags = tags[...].astype(f32)
+    own_docs = jnp.where(lane < HEAD_SIZE // 2, own_tags, 0.0).astype(jnp.bfloat16)
+    nt = (((1,), (1,)), ((), ()))
+    same = lax.dot_general(
+        own_docs, kv[:, 2 * kv_width :], nt, preferred_element_type=f32
+    )
+    position = me * rows + lax.broadcasted_iota(jnp.int32, same.shape, 0)
+    key_position = lax.broadcasted_iota(jnp.int32, same.shape, 1)
+    same = jnp.where(key_position <= position, same, 0.0)
+    visible = jnp.concatenate([same] * heads, axis=0) > 0.5
+    square = jnp.zeros((rows, 1), f32)
+    for g in range(group_count):
+        first = g * heads * HEAD_SIZE
+        stacked = jnp.concatenate(
+            [queries[:, first + h * HEAD_SIZE : first + (h + 1) * HEAD_SIZE] for h in range(heads)],
+            axis=0,
+        )
+        scores = lax.dot_general(
+            stacked, kv[:, g * HEAD_SIZE : (g + 1) * HEAD_SIZE], nt, preferred_element_type=f32
+        ) * (1.0 / math.sqrt(HEAD_SIZE))
+        masked = jnp.where(visible, scores, NEG)
+        top = jnp.max(masked, axis=1, keepdims=True)
+        weights = jnp.where(visible, jnp.exp(masked - top), 0.0)
+        total = jnp.sum(weights, axis=1, keepdims=True)
+        attended = jnp.dot(
+            weights.astype(jnp.bfloat16),
+            kv[:, kv_width + g * HEAD_SIZE : kv_width + (g + 1) * HEAD_SIZE],
+            preferred_element_type=f32,
+        ) / total
+        for h in range(heads):
+            part_cols = pl.ds(first + h * HEAD_SIZE, HEAD_SIZE)
+            low = (
+                hidden[:, part_cols].astype(f32) + attended[h * rows : (h + 1) * rows]
+            ).astype(jnp.bfloat16)
+            resid[:, part_cols] = low
+            wide = low.astype(f32)
+            square = square + jnp.sum(wide * wide, axis=1, keepdims=True)
+    scale = lax.rsqrt(square * (1.0 / width) + 1e-06)
+    image_row = own_tags[:, HEAD_SIZE - 1 :] > 0.5
+    for c in range(width // COLS):
+        part_cols = pl.ds(c * COLS, COLS)
+        gain = jnp.where(image_row, gains[1:2, part_cols], gains[0:1, part_cols])
+        normed[:, part_cols] = (
+            resid[:, part_cols].astype(f32) * scale * gain
+        ).astype(jnp.bfloat16)
+
+    target = jnp.where(me * mp_size + z >= FF // units, 1.0, 0.0)
     row_chunks = rows // CHUNK
 
     def place(seq_index, k):
@@ -156,7 +227,9 @@
                 here, ring[slot, 1, :size, :], last_dims, preferred_element_type=f32
             )
             value = gate / (1.0 + jnp.exp(-gate)) * up
-            value = jnp.where(wanted[rows_at(i), :1] > 0.5, value, 0.0)
+            value = jnp.where(
+                jnp.abs(kv[rows_at(i), kv.shape[1] - 1 :].astype(f32) - target) < 0.5, value, 0.0
+            )
             act[rows_at(i), pl.ds(offset, size)] = value.astype(jnp.bfloat16)
             return carry
 
@@ -289,8 +362,10 @@
             left_copy(k).wait_send()
 
 
-def feed_forward(normed, residual, wanted, input_weights, output_weights, seq_size, mp_size):
-    rows, width = residual.shape
+def layer(
+    queries, keys, values, tags, hidden, gains, input_weights, output_weights, seq_size, mp_size
+):
+    rows, width = queries.shape
     total_rows = rows * seq_size
     units = output_weights.shape[0]
     chips = seq_size // 2
@@ -307,9 +382,13 @@
     return pl.pallas_call(
         functools.partial(ffn_kernel, seq_size, mp_size),
         out_shape=jax.ShapeDtypeStruct((rows, width), bf16),
-        in_specs=[vmem, vmem, vmem, hbm, hbm],
+        in_specs=[vmem] * 6 + [hbm, hbm],
         out_specs=vmem,
         scratch_shapes=[
+            pltpu.VMEM((total_rows, 2 * keys.shape[1] + HEAD_SIZE), bf16),
+            pltpu.VMEM((rows, width), bf16),
+            pltpu.VMEM((rows, width), bf16),
+            dma((seq_size - 1, 3)), dma((seq_size - 1, 3)),
             pltpu.VMEM((total_rows, width), bf16),
             pltpu.VMEM((slots, 2, tiles[0][1], width), bf16),
             pltpu.VMEM((units, width), bf16),
@@ -337,75 +416,22 @@
         cost_estimate=pl.CostEstimate(
             flops=flops, bytes_accessed=6 * units * width, transcendentals=0
         ),
-        name="feed_forward",
-    )(normed, residual, wanted, input_weights, output_weights)
-
-
-def attend(queries, payload, all_payload, hidden_in, shard_index):
-    row_count = queries.shape[0]
-    kv_width = (payload.shape[1] - HEAD_SIZE) // 2
-    group_count = kv_width // HEAD_SIZE
-    head_count = queries.shape[1] // HEAD_SIZE
-    total_rows = all_payload.shape[0]
-    query_by_group = queries.reshape(
-        row_count, group_count, head_count // group_count, HEAD_SIZE
-    )
-    key_by_group = all_payload[:, :kv_width].reshape(total_rows, group_count, HEAD_SIZE)
-    value_by_group = all_payload[:, kv_width : 2 * kv_width].reshape(
-        total_rows, group_count, HEAD_SIZE
-    )
-    scores = jnp.einsum(
-        "rgqd,ngd->rgqn", query_by_group, key_by_group, preferred_element_type=jnp.float32
-    ) * (1.0 / math.sqrt(HEAD_SIZE))
-    position = shard_index * row_count + jnp.arange(row_count, dtype=jnp.int32)
-    key_position = jnp.arange(total_rows, dtype=jnp.int32)
-    own_doc = payload[:, 2 * kv_width]
-    key_doc = all_payload[:, 2 * kv_width]
-    visible = (own_doc[:, None] == key_doc[None, :]) & (
-        key_position[None, :] <= position[:, None]
-    )
-    visible = visible[:, None, None, :]
-    masked = jnp.where(visible, scores, NEG)
-    row_max = jnp.max(masked, axis=-1)
-    weights = jnp.where(visible, jnp.exp(masked - row_max[..., None]), 0.0)
-    total = jnp.sum(weights, axis=-1)
-    weighted = jnp.einsum(
-        "rgqn,ngd->rgqd",
-        weights.astype(jnp.bfloat16),
-        value_by_group,
-        preferred_element_type=jnp.float32,
-    )
-    attended = (weighted / total[..., None]).reshape(row_count, head_count * HEAD_SIZE)
-    return (hidden_in.astype(jnp.float32) + attended).astype(jnp.bfloat16)
-
-
-def normalise(residual, modality, norm_gains):
-    wide = residual.astype(jnp.float32)
-    mean_square = jnp.mean(wide * wide, axis=-1, keepdims=True)
-    gain = jnp.where(modality[:, None] == 1, norm_gains[1][None, :], norm_gains[0][None, :])
-    return (wide * lax.rsqrt(mean_square + 1e-06) * gain).astype(jnp.bfloat16)
+        name="layer",
+    )(queries, keys, values, tags, hidden, gains, input_weights, output_weights)
 
 
 def body(
     seq_size, mp_size,
     queries, keys, values, hidden_in, doc_ids, modality, input_weights, output_weights, norm_gains
 ):
-    row_count = queries.shape[0]
-    kv_width = keys.shape[1]
-    shard_index = lax.axis_index("seq")
-    device_index = shard_index * mp_size + lax.axis_index("mp")
     lane = jnp.arange(HEAD_SIZE, dtype=jnp.int32)[None, :]
-    tags = jnp.where(lane == 0, doc_ids[:, None], jnp.where(lane == 1, modality[:, None], 0))
-    payload = jnp.concatenate([keys, values, tags.astype(jnp.bfloat16)], axis=1)
-    all_payload = lax.all_gather(payload, "seq", axis=0, tiled=True)
-    residual = attend(queries, payload, all_payload, hidden_in, shard_index)
-    normed = normalise(residual, modality, norm_gains)
-    is_image = device_index >= FF // output_weights.shape[0]
-    wanted = (all_payload[:, 2 * kv_width + 1] > 0.5) == is_image
-    wanted = jnp.broadcast_to(wanted[:, None], (wanted.shape[0], HEAD_SIZE)).astype(jnp.float32)
+    tags = jnp.where(
+        lane < HEAD_SIZE // 2, lane == doc_ids[:, None], modality[:, None] == 1
+    ).astype(jnp.bfloat16)
     by_unit = jnp.transpose(input_weights, (1, 2, 0))
-    return feed_forward(
-        normed, residual, wanted, by_unit, output_weights, seq_size, mp_size
+    return layer(
+        queries, keys, values, tags, hidden_in, norm_gains, by_unit, output_weights,
+        seq_size, mp_size,
     )
 
 

time: 103 us -> 92.7 us (0.900)
  Pallas kernels: 78.7 us -> 88.6 us
  blocking collectives: 8.98 us -> 0 us
  local copies, waits for them, and re-layouts: 6.74 us -> 1.82 us
  matrix products: 3.43 us -> 0 us
  other arithmetic: 4.36 us -> 2.01 us
    pallas_call x1, Pallas kernels: 78.7 us -> 88.6 us  [layer(): pl.pallas_call(functools.partial(ffn_kernel, seq_size, mp_size), out_shap...]
    all_gather x1 -> x0, blocking collectives: 8.98 us -> none  [body(): all_payload = lax.all_gather(payload, 'seq', axis=0, tiled=True)]
    dot_general x2 -> x0, matrix products: 1.95 us -> none  [the longest x1 1.56 us: attend(): jnp.einsum('rgqn,ngd->rgqd', weights.astype(jnp.bfloat16), value_by_group...]
    slice x4 -> x0, local copies, waits for them, and re-layouts: 1.78 us -> none  [the longest x1 1.51 us: normalise(): norm_gains[1][None, :]]
    sub x1 -> x0, matrix products: 1.49 us -> none  [attend(): weights = jnp.where(visible, jnp.exp(masked - row_max[..., None]), 0.0)]
    unnamed x15 -> x1, local copies, waits for them, and re-layouts: 2.9 us -> 1.82 us
where the time goes in v3:
time: 92.7 us; the launch traced here: 92.5 us
  Pallas kernels  88.6 us (96%)
  other arithmetic  2.01 us (2%)
  local copies, waits for them, and re-layouts  1.82 us (2%)
    pallas_call x1, Pallas kernels, layer(): pl.pallas_call(functools.partial(ffn_kernel, seq_size, mp_size), out_shap...  88.6 us

profile of v3, /device:TPU:0, one launch (start us, length us, event | category | flops | bytes accessed | tf_op | source)
XLA Modules:
  0.0 92.5 jit_solution(3988810339741831469)
XLA Ops:
  0.0 0.7 broadcast_compare_fusion
  0.7 1.3 %fusion.1.tags = bf16[64,128]{1,0:T(8,128)(2,1)} fusion(s32[64]{0:T(128)} %param.13, pred[64]{0:T(512)(128)(4,1)S(1)} %broadcast_compare_fusion, pred[128]{0:T(512)(128)(4,1)S(1)} %iota_compare_fusion.1), kind=kLoop, calls=%fused_computation.2 | loop fusion | flops 24576 | bytes 16832 | tf_op jit(solution)/shard_map/convert_element_type | solution.py:430
  2.0 88.6 %layer.1 = bf16[64,3584]{1,0:T(8,128)(2,1)} custom-call(bf16[64,3584]{1,0:T(8,128)(2,1)} %queries.1, bf16[64,512]{1,0:T(8,128)(2,1)} %keys.1, bf16[64,512]{1,0:T(8,128)(2,1)} %values.1, bf16[64,128]{1,0:T(8,128)(2,1)} %fusion.1.tags, bf16[64,3584]{1,0:T(8,128)(2,1)} %hidden.1, f32[2,3584]{1,0:T(2,128)} %gains.1, bf16[2,2368,3584]{2,1,0:T(8,128)(2,1)} %bitcast.1, ...), custom_call_target="tpu_custom_call" | custom-call | flops 13035896832 | bytes 50921472 | tf_op jit(solution)/shard_map/layer/pallas_call | solution.py:382
  90.6 1.8 %copy.11 = bf16[64,3584]{1,0:T(8,128)(2,1)} copy(bf16[64,3584]{1,0:T(8,128)(2,1)} %layer.1) | data formatting | bytes 917504
  (1 shorter events, 0.0 us)

commit v4 on v3

--- a/solution.py
+++ b/solution.py
@@ -16,6 +16,7 @@
 ROW_TILE = 256
 SLOTS = 6
 LAG = 2
+SKEW = 3
 NEG = -1e30
 
 
@@ -279,22 +280,6 @@
             ).astype(jnp.bfloat16)
             cross_copy(d, k).start()
 
-    order = list(range(1, chips)) + [0]
-    for k in range(chunks):
-
-        def down(i, carry, k=k):
-            part[k, rows_at(i), :] = jnp.dot(
-                act[rows_at(i), :], w_down[:, cols(k)], preferred_element_type=f32
-            ).astype(jnp.bfloat16)
-            return carry
-
-        lax.fori_loop(0, blocks, down, 0)
-        for d in order:
-            pair_copy(d, k).start()
-        if k > 0:
-            cross_stage(k - 1)
-    cross_stage(chunks - 1)
-
     def gather_own(k):
         pair_copy(0, k).wait_recv()
         total = part[k, block_of(me), :].astype(f32) + pair_recv[k, 0].astype(f32)
@@ -324,28 +309,61 @@
             left_copy(k).start()
 
     low_half = z * 2 < mp_size
-    for t in range(chunks + LAG):
+    edge = jnp.logical_or(z == 0, z == mp_size - 1)
+
+    def finish(k):
+        ffn = own[k] + right_recv[k].astype(f32) + left_recv[k].astype(f32)
+        out[:, cols(k)] = (resid[:, cols(k)].astype(f32) + ffn).astype(jnp.bfloat16)
+
+    def near_step(k):
+        gather_own(k)
+
+        @pl.when(low_half)
+        def _():
+            step_right(k)
+
+        @pl.when(jnp.logical_not(low_half))
+        def _():
+            step_left(k)
+
+    def far_step(k):
+        @pl.when(low_half)
+        def _():
+            step_left(k)
+
+        @pl.when(jnp.logical_not(low_half))
+        def _():
+            step_right(k)
+
+        finish(k)
+
+    order = list(range(1, chips)) + [0]
+    for t in range(chunks + LAG + SKEW):
         if t < chunks:
-            gather_own(t)
-
-        @pl.when(low_half)
-        def _():
-            if t < chunks:
-                step_right(t)
-            if t >= LAG:
-                step_left(t - LAG)
-
-        @pl.when(jnp.logical_not(low_half))
-        def _():
-            if t < chunks:
-                step_left(t)
-            if t >= LAG:
-                step_right(t - LAG)
-
-        if t >= LAG:
-            k = t - LAG
-            ffn = own[k] + right_recv[k].astype(f32) + left_recv[k].astype(f32)
-            out[:, cols(k)] = (resid[:, cols(k)].astype(f32) + ffn).astype(jnp.bfloat16)
+
+            def down(i, carry, k=t):
+                part[k, rows_at(i), :] = jnp.dot(
+                    act[rows_at(i), :], w_down[:, cols(k)], preferred_element_type=f32
+                ).astype(jnp.bfloat16)
+                return carry
+
+            lax.fori_loop(0, blocks, down, 0)
+            for d in order:
+                pair_copy(d, t).start()
+        if 1 <= t <= chunks:
+            cross_stage(t - 1)
+        if SKEW <= t < chunks + SKEW:
+            near_step(t - SKEW)
+        if t >= LAG + SKEW:
+
+            @pl.when(jnp.logical_not(edge))
+            def _(k=t - LAG - SKEW):
+                far_step(k)
+
+    @pl.when(edge)
+    def _():
+        for k in range(chunks):
+            far_step(k)
 
     for k in range(chunks):
         for d in range(chips):

time: 92.7 us -> 70.4 us (0.76)
  Pallas kernels: 88.6 us -> 66.4 us
    pallas_call x1, Pallas kernels: 88.6 us -> 66.4 us  [layer(): pl.pallas_call(functools.partial(ffn_kernel, seq_size, mp_size), out_shap...]
where the time goes in v4:
time: 70.4 us; the launch traced here: 70.2 us
  Pallas kernels  66.4 us (94%)
  other arithmetic  2.01 us (3%)
  local copies, waits for them, and re-layouts  1.82 us (3%)
    pallas_call x1, Pallas kernels, layer(): pl.pallas_call(functools.partial(ffn_kernel, seq_size, mp_size), out_shap...  66.4 us
    unnamed x1, local copies, waits for them, and re-layouts  1.82 us

profile of v4, /device:TPU:0, one launch (start us, length us, event | category | flops | bytes accessed | tf_op | source)
XLA Modules:
  0.0 70.2 jit_solution(8401748036431150226)
XLA Ops:
  0.0 0.7 broadcast_compare_fusion
  0.7 1.3 %fusion.1.tags = bf16[64,128]{1,0:T(8,128)(2,1)} fusion(s32[64]{0:T(128)} %param.13, pred[64]{0:T(512)(128)(4,1)S(1)} %broadcast_compare_fusion, pred[128]{0:T(512)(128)(4,1)S(1)} %iota_compare_fusion.1), kind=kLoop, calls=%fused_computation.2 | loop fusion | flops 24576 | bytes 16832 | tf_op jit(solution)/shard_map/convert_element_type | solution.py:448
  2.0 66.4 %layer.1 = bf16[64,3584]{1,0:T(8,128)(2,1)} custom-call(bf16[64,3584]{1,0:T(8,128)(2,1)} %queries.1, bf16[64,512]{1,0:T(8,128)(2,1)} %keys.1, bf16[64,512]{1,0:T(8,128)(2,1)} %values.1, bf16[64,128]{1,0:T(8,128)(2,1)} %fusion.1.tags, bf16[64,3584]{1,0:T(8,128)(2,1)} %hidden.1, f32[2,3584]{1,0:T(2,128)} %gains.1, bf16[2,2368,3584]{2,1,0:T(8,128)(2,1)} %bitcast.1, ...), custom_call_target="tpu_custom_call" | custom-call | flops 13035896832 | bytes 50921472 | tf_op jit(solution)/shard_map/layer/pallas_call | solution.py:400
  68.4 1.8 %copy.11 = bf16[64,3584]{1,0:T(8,128)(2,1)} copy(bf16[64,3584]{1,0:T(8,128)(2,1)} %layer.1) | data formatting | bytes 917504
  (1 shorter events, 0.0 us)
